TPU v7x, 512 devices: a whole 4x4x16 slice. The times are simulated.
512 devices in a mesh: row: 8 (over y, z_hi), col: 64 (over z_lo, x, core).
Axes of the slice: x: 4, y: 4, z: 16 (z_hi: 2, z_lo: 8; z = z_hi * 8 + z_lo), core: 2. Of those that a mesh axis runs over, the one named last changes fastest.
Arguments:
- side_a: float32 [64, 8192], P('row', 'col'), may hold values from -6 to 6
- side_b: float32 [2048, 8192], P('col', 'row'), may hold values from -6 to 6
- pair_grad: float32 [64, 2048, 128], P('row', 'col'), may hold values from -6 to 6
- out_weight: float32 [1024, 128], replicated, may hold values from -0.1875 to 0.1875
Outputs:
- grad_a: float32 [64, 8192], P('row', 'col')
- grad_b: float32 [2048, 8192], P('col', 'row')
- grad_weight: float32 [1024, 128], replicated
- grad_bias: float32 [128], replicated
All inputs are finite; a program needn't handle non-finite values.
Results may differ from a plain program's by a relative error of at most 0.00013.
Values sent between devices are 32-bit elements; how exact they have to be, the bound alone decides.
A program may use at most 64 MiB of HBM per device.

v0:
```python
import jax
import jax.numpy as jnp
from jax import lax
from jax.sharding import PartitionSpec as P

S = 256
C = 32
P_SIZE = 128


def local(side_a, side_b, pair_grad, out_weight):
    high = lax.Precision.HIGHEST
    rows = pair_grad.shape[0]
    cols = pair_grad.shape[1]
    left = lax.all_gather(side_a, "col", axis=1, tiled=True).reshape(rows, S, C)
    right = lax.all_gather(side_b, "row", axis=1, tiled=True).reshape(cols, S, C)
    left_flat = jnp.transpose(left, (0, 2, 1)).reshape(rows * C, S)
    right_flat = jnp.transpose(right, (1, 0, 2)).reshape(S, cols * C)
    flat_pair = pair_grad.reshape(rows * cols, P_SIZE)
    grad_outer = jnp.dot(flat_pair, out_weight.T, precision=high)
    grad_tile = jnp.transpose(grad_outer.reshape(rows, cols, C, C), (0, 2, 1, 3)).reshape(
        rows * C, cols * C
    )
    left_grad = jnp.dot(grad_tile, right_flat.T, precision=high) / S
    left_part = jnp.transpose(left_grad.reshape(rows, C, S), (0, 2, 1)).reshape(rows, S * C)
    right_grad = jnp.dot(left_flat.T, grad_tile, precision=high) / S
    right_part = jnp.transpose(right_grad.reshape(S, cols, C), (1, 0, 2)).reshape(cols, S * C)
    left_total = lax.psum(left_part, "col")
    right_total = lax.psum(right_part, "row")
    left_width = side_a.shape[1]
    right_width = side_b.shape[1]
    grad_a = lax.dynamic_slice_in_dim(left_total, lax.axis_index("col") * left_width, left_width, 1)
    grad_b = lax.dynamic_slice_in_dim(
        right_total, lax.axis_index("row") * right_width, right_width, 1
    )
    outer = jnp.dot(left_flat, right_flat, precision=high) / S
    outer = jnp.transpose(outer.reshape(rows, C, cols, C), (0, 2, 1, 3)).reshape(rows * cols, C * C)
    weight_part = jnp.dot(outer.T, flat_pair, precision=high)
    bias_part = jnp.sum(flat_pair, axis=0)
    weight_sums = lax.psum((weight_part, bias_part), ("row", "col"))
    return (grad_a, grad_b, weight_sums[0], weight_sums[1])


def solution(mesh):
    in_specs = (P("row", "col"), P("col", "row"), P("row", "col", None), P())
    out_specs = (P("row", "col"), P("col", "row"), P(), P())
    return jax.shard_map(local, mesh=mesh, in_specs=in_specs, out_specs=out_specs, check_vma=False)
```

profile of v0, /device:TPU:4, one launch (start us, length us, event | category | flops | bytes accessed | tf_op | source)
XLA Modules:
  0.0 1648.9 jit_solution(14450162567662222692)
XLA Ops:
  7.2 0.0 all-gather.2.cloned.1.call-start
  7.2 0.7 all-gather.2.cloned.1.call-update
  7.9 0.0 all-reduce.6.cloned.1.call-start
  8.0 0.3 copy-done
  8.2 5.9 convolution_bitcast_fusion
  14.1 3.7 reshape.48
  17.9 119.1 %all_gather.7 = f32[8,8192]{1,0:T(8,128)S(1)} all-gather(f32[8,128]{1,0:T(8,128)S(1)} %copy-done.2), channel_id=1, replica_groups=mesh['row'=8,'col'=64] {'col'}, dimensions={1}, use_global_device_ids=true | all-gather | bytes 266240 | tf_op jit(solution)/shard_map/all_gather | solution.py:15
  137.0 0.3 reshape.53
  137.3 0.3 copy.12
  137.6 1.8 convolution_multiply_fusion.1
  139.5 2.6 copy.13
  142.1 4.4 reshape.56
  146.5 0.2 all-reduce.4.cloned.1.call-start
  146.8 3.7 reshape.49
  150.5 2.8 copy.10
  153.3 1.0 convolution_multiply_fusion.2
  154.4 0.3 copy.11
  154.7 1.2 reshape.52
  155.9 1.0 convolution_multiply_fusion
  157.0 2.7 reshape.57
  159.7 6.5 copy.17
  166.2 3.8 reshape.58
  170.0 0.0 all-reduce.8.cloned.1.call-start
  170.1 2.6 fusion.1
  172.7 0.1 reduce_sum.9
  172.8 158.6 %psum.31 = f32[128]{0:T(128)} all-reduce(f32[128]{0:T(128)S(1)} %reduce_sum.9), channel_id=1, replica_groups=mesh['row'=8,'col'=64] {'row','col'}, use_global_device_ids=true, to_apply=%region_4.0 | all-reduce | flops 128 | bytes 1024 | tf_op jit(solution)/shard_map/psum | solution.py:40
  331.4 64.2 %all-reduce.6.cloned.1.call-done = f32[32,8192]{1,0:T(8,128)} async-done(((f32[32,8192]{1,0:T(8,128)}), f32[32,8192]{1,0:T(8,128)}) %all-reduce.6.cloned.1.call-update) | async-done | bytes 1048592 | tf_op jit(solution)/shard_map/psum | solution.py:29
  395.6 1.6 constant_dynamic-slice_fusion
  397.2 767.8 %all-reduce.4.cloned.1.call-done = f32[8,8192]{1,0:T(8,128)} async-done(((f32[8,8192]{1,0:T(8,128)}), f32[8,8192]{1,0:T(8,128)}) %all-reduce.4.cloned.1.call-update) | async-done | bytes 262160 | tf_op jit(solution)/shard_map/psum | solution.py:28
  1165.0 1.3 constant_dynamic-slice_fusion.1
  1166.3 474.2 %all-reduce.8.cloned.1.call-done = f32[1024,128]{1,0:T(8,128)} async-done(((f32[1024,128]{1,0:T(8,128)}), f32[1024,128]{1,0:T(8,128)}) %all-reduce.8.cloned.1.call-update) | async-done | bytes 524304 | tf_op jit(solution)/shard_map/psum | solution.py:40
  1640.5 1.9 copy.21
  (9 shorter events, 0.1 us)
Async XLA Ops:
  7.2 1.0 copy-start
  7.2 139.6 %all-gather.2.cloned.1.call-start = ((), (), s32[]{:S(2)}) async-start(), calls=%async_computation | async-start | bytes 1179648 | tf_op jit(solution)/shard_map/all_gather | solution.py:16
  7.9 387.7 %all-reduce.6.cloned.1.call-start = ((), (), s32[]{:S(2)}) async-start(), calls=%async_computation.2 | async-start | bytes 2097152 | tf_op jit(solution)/shard_map/psum | solution.py:29
  8.2 9.7 copy-start.2
  146.5 1018.5 %all-reduce.4.cloned.1.call-start = ((), (), s32[]{:S(2)}) async-start(), calls=%async_computation.1 | async-start | bytes 524288 | tf_op jit(solution)/shard_map/psum | solution.py:28
  166.2 3.9 copy-start.1
  170.0 1470.4 %all-reduce.8.cloned.1.call-start = ((), (), s32[]{:S(2)}) async-start(), calls=%async_computation.3 | async-start | bytes 1048576 | tf_op jit(solution)/shard_map/psum | solution.py:40
Sparse Core Ops, SparseCore 0:
  11.2 95.5 all-gather.1
  146.6 248.9 all-reduce.5
  398.5 766.4 all-reduce.3
  1171.8 468.6 all-reduce.7
where the time goes:
time: 1650 us
  waiting for transfers between devices  1310 us (79%)
  blocking collectives  278 us (17%)
  local copies, waits for them, and re-layouts  37.5 us (2%)
    psum x1, waiting for transfers between devices, local(): left_total = lax.psum(left_part, 'col')  768 us
    psum x1, waiting for transfers between devices, local(): weight_sums = lax.psum((weight_part, bias_part), ('row', 'col'))  474 us
    psum x1, blocking collectives, local(): weight_sums = lax.psum((weight_part, bias_part), ('row', 'col'))  159 us
    all_gather x1, blocking collectives, local(): left = lax.all_gather(side_a, 'col', axis=1, tiled=True).reshape(rows, S, C)  119 us
    psum x1, waiting for transfers between devices, local(): right_total = lax.psum(right_part, 'row')  64.2 us
  transfers between devices with their start and end apart: 4, of which 3 were waited for; matrix products, arithmetic and copies ran while one was open for 3% of the time, Pallas kernels for 0%

commit v1 on v0

--- a/solution.py
+++ b/solution.py
@@ -37,7 +37,7 @@
     outer = jnp.transpose(outer.reshape(rows, C, cols, C), (0, 2, 1, 3)).reshape(rows * cols, C * C)
     weight_part = jnp.dot(outer.T, flat_pair, precision=high)
     bias_part = jnp.sum(flat_pair, axis=0)
-    weight_sums = lax.psum((weight_part, bias_part), ("row", "col"))
+    weight_sums = lax.psum(lax.psum((weight_part, bias_part), "row"), "col")
     return (grad_a, grad_b, weight_sums[0], weight_sums[1])
 
 

time: 1650 us -> 1310 us (0.79)
  the two profiles are of different devices: /device:TPU:4 before, /device:TPU:8 now
where the time goes in v1:
time: 1310 us
  waiting for transfers between devices  853 us (65%)
  blocking collectives  389 us (30%)
  local copies, waits for them, and re-layouts  39.3 us (3%)
  matrix products  14.6 us (1%)
  between operations  13.8 us (1%)
    psum x1, waiting for transfers between devices, local(): left_total = lax.psum(left_part, 'col')  561 us
    psum x1, waiting for transfers between devices, local(): weight_sums = lax.psum(lax.psum((weight_part, bias_part), 'row'), 'col')  292 us
    psum x2, blocking collectives, local(): weight_sums = lax.psum(lax.psum((weight_part, bias_part), 'row'), 'col')  253 us
    all_gather x1, blocking collectives, local(): left = lax.all_gather(side_a, 'col', axis=1, tiled=True).reshape(rows, S, C)  136 us
  transfers between devices with their start and end apart: 3, of which 2 were waited for; matrix products, arithmetic and copies ran while one was open for 2% of the time, Pallas kernels for 0%

profile of v1, /device:TPU:8, one launch (start us, length us, event | category | flops | bytes accessed | tf_op | source)
XLA Modules:
  0.0 1309.9 jit_solution(11231832324733738134)
XLA Ops:
  7.2 0.0 all-gather.2.cloned.1.call-start
  7.2 0.7 all-gather.2.cloned.1.call-update
  7.9 0.0 all-reduce.7.cloned.1.call-start
  8.0 135.9 %all_gather.7 = f32[8,8192]{1,0:T(8,128)S(1)} all-gather(f32[8,128]{1,0:T(8,128)} %param.4), channel_id=1, replica_groups=mesh['row'=8,'col'=64] {'col'}, dimensions={1}, use_global_device_ids=true | all-gather | bytes 266240 | tf_op jit(solution)/shard_map/all_gather | solution.py:15
  143.9 0.3 reshape.53
  144.2 0.3 copy.12
  144.6 5.9 convolution_bitcast_fusion
  150.5 3.7 reshape.48
  154.2 1.8 convolution_multiply_fusion.1
  156.1 2.6 copy.13
  158.7 4.4 reshape.56
  163.1 3.7 reshape.49
  166.8 2.8 copy.10
  169.6 2.0 convolution_multiply_fusion
  171.6 3.9 reshape.57
  175.6 6.5 copy.17
  182.1 4.6 reshape.58
  186.7 3.8 fusion.1
  190.5 0.0 all-reduce.7.cloned.1.call-update
  190.6 0.0 all-reduce.5.cloned.1.call-start
  190.6 1.0 convolution_multiply_fusion.2
  191.6 0.3 copy.11
  192.0 1.2 reshape.52
  193.2 291.8 %all-reduce.7.cloned.1.call-done = (f32[1024,128]{1,0:T(8,128)}, f32[32,8192]{1,0:T(8,128)}) async-done(((f32[1024,128]{1,0:T(8,128)}, f32[32,8192]{1,0:T(8,128)}), (f32[1024,128]{1,0:T(8,128)}, f32[32,8192]{1,0:T(8,128)})) %all-reduce.7.cloned.1.call-update) | async-done | bytes 1572880 | tf_op jit(solution)/shard_map/psum | solution.py:40
  485.0 0.0 all-reduce.5.cloned.1.call-update
  485.0 0.1 reduce_sum.9
  485.1 41.9 %psum.46 = f32[128]{0:T(128)S(1)} all-reduce(f32[128]{0:T(128)S(1)} %reduce_sum.9), channel_id=1, replica_groups=mesh['row'=8,'col'=64] {'row'}, use_global_device_ids=true, to_apply=%region_5.0 | all-reduce | flops 128 | bytes 1024 | tf_op jit(solution)/shard_map/psum | solution.py:40
  527.0 210.8 %psum.47 = f32[128]{0:T(128)} all-reduce(f32[128]{0:T(128)S(1)} %psum.46), channel_id=1, replica_groups=mesh['row'=8,'col'=64] {'col'}, use_global_device_ids=true, to_apply=%region_6.0 | all-reduce | flops 128 | bytes 1024 | tf_op jit(solution)/shard_map/psum | solution.py:40
  737.8 1.6 constant_dynamic-slice_fusion
  739.4 560.8 %all-reduce.5.cloned.1.call-done = (f32[8,8192]{1,0:T(8,128)}, f32[1024,128]{1,0:T(8,128)}) async-done(((f32[8,8192]{1,0:T(8,128)}, f32[1024,128]{1,0:T(8,128)}), (f32[8,8192]{1,0:T(8,128)}, f32[1024,128]{1,0:T(8,128)})) %all-reduce.5.cloned.1.call-update) | async-done | bytes 786448 | tf_op jit(solution)/shard_map/psum | solution.py:28
  1300.2 1.3 constant_dynamic-slice_fusion.1
  1301.5 1.9 copy.22
  (5 shorter events, 0.0 us)
Async XLA Ops:
  7.2 137.4 %copy-start = (f32[1024,128]{1,0:T(8,128)S(1)}, f32[1024,128]{1,0:T(8,128)}, u32[]{:S(2)}) copy-start(f32[1024,128]{1,0:T(8,128)} %param.7) | copy-start | bytes 1572868
  7.2 155.9 %all-gather.2.cloned.1.call-start = ((), (), s32[]{:S(2)}) async-start(), calls=%async_computation | async-start | bytes 1179648 | tf_op jit(solution)/shard_map/all_gather | solution.py:16
  7.9 477.1 %all-reduce.7.cloned.1.call-start = ((), (), s32[]{:S(2)}) async-start(), calls=%async_computation.2 | async-start | bytes 3145728 | tf_op jit(solution)/shard_map/psum | solution.py:40
  182.1 4.6 copy-start.1
  190.6 1109.7 %all-reduce.5.cloned.1.call-start = ((), (), s32[]{:S(2)}) async-start(), calls=%async_computation.1 | async-start | bytes 1572864 | tf_op jit(solution)/shard_map/psum | solution.py:28
Sparse Core Ops, SparseCore 0:
  11.2 95.3 all-gather.1
  190.7 294.2 all-reduce.6
  488.0 812.2 all-reduce.4
